TPU v7x, 32 devices: a whole 2x2x4 slice. The times are simulated.
32 devices in a mesh: pair: 2 (over x), dp: 2 (over y), vocab: 8 (over z, core).
Axes of the slice: x: 2, y: 2, z: 4, core: 2. Of those that a mesh axis runs over, the one named last changes fastest.
Arguments:
- hidden: bfloat16 [2, 48, 8192], P(None, None, ('pair', 'dp')), may hold values from -64 to 64
- head_weight: bfloat16 [8192, 16384], P(('pair', 'dp'), 'vocab'), may hold values from -2 to 2
- answer_mask: int32 [48], replicated, may hold values 0 or 1
Outputs:
- grad_hidden: float32 [96, 8192], P('vocab', ('pair', 'dp'))
- kl_rows: float32 [48], P('dp')
All inputs are finite; a program needn't handle non-finite values.
Results may differ from a plain program's by a relative error of at most 0.0003.
Values sent between devices are 32-bit elements; how exact they have to be, the bound alone decides.
A program may use at most 64 MiB of HBM per device.

v0:
```python
import jax
import jax.numpy as jnp
from jax import lax
from jax.sharding import PartitionSpec as P

trades_scale = 6.0


def from_partner(value, axis, bit):
    mask = 2**bit
    pairs = [(source, source ^ mask) for source in range(lax.axis_size(axis))]
    return lax.ppermute(value, axis, pairs)


def per_device(hidden, head_weight, answer_mask):
    flat = hidden.reshape(-1, hidden.shape[2])
    all_rows = flat.shape[0]
    tokens_total = all_rows // 2
    tok_group = tokens_total // lax.axis_size("dp")
    mask_float = answer_mask.astype(jnp.float32)
    weights_all = trades_scale * mask_float
    start_row = lax.axis_index("dp") * tok_group
    head_wide = head_weight.astype(jnp.float32)
    own_logits = lax.psum_scatter(
        jnp.dot(flat, head_weight, preferred_element_type=jnp.float32),
        ("pair", "dp"),
        scatter_dimension=0,
        tiled=True,
    )
    is_clean = lax.axis_index("pair") == 0
    row_top = lax.pmax(jnp.max(own_logits, axis=1), "vocab")
    row_total = lax.psum(jnp.sum(jnp.exp(own_logits - row_top[:, None]), axis=1), "vocab")
    own_logp = own_logits - (row_top + jnp.log(row_total))[:, None]
    other_logp = from_partner(own_logp, "pair", 0)
    clean_logp = jnp.where(is_clean, own_logp, other_logp)
    adv_logp = jnp.where(is_clean, other_logp, own_logp)
    clean_prob = jnp.exp(clean_logp)
    kl_values = lax.psum(jnp.sum(clean_prob * (clean_logp - adv_logp), axis=1), "vocab")
    row_weight = lax.dynamic_slice_in_dim(weights_all, start_row, tok_group)[:, None]
    clean_grad = row_weight * clean_prob * (clean_logp - adv_logp - kl_values[:, None])
    adv_grad = row_weight * (jnp.exp(adv_logp) - clean_prob)
    logit_grad = jnp.where(is_clean, clean_grad, adv_grad)
    partial_grad = lax.dot_general(
        lax.all_gather(logit_grad, ("pair", "dp"), axis=0, tiled=True),
        head_wide,
        (((1,), (1,)), ((), ())),
        precision=lax.Precision.HIGHEST,
        preferred_element_type=jnp.float32,
    )
    kl_out = kl_values * lax.dynamic_slice_in_dim(mask_float, start_row, tok_group)
    grad_rows = lax.psum_scatter(partial_grad, "vocab", scatter_dimension=0, tiled=True)
    return (grad_rows, kl_out)


def solution(mesh):
    return jax.shard_map(
        per_device,
        mesh=mesh,
        in_specs=(P(None, None, ("pair", "dp")), P(("pair", "dp"), "vocab"), P()),
        out_specs=(P("vocab", ("pair", "dp")), P("dp")),
        check_vma=False,
    )
```

profile of v0, /device:TPU:0, one launch (start us, length us, event | category | flops | bytes accessed | tf_op | source)
XLA Modules:
  0.0 153.2 jit_solution(2676586459246010135)
XLA Ops:
  7.2 0.0 copy-start
  7.2 0.0 reduce-scatter.6.cloned.1.call-start
  7.2 0.9 copy-done
  8.2 0.0 copy-start.2
  8.2 0.0 copy-start.1
  8.2 5.7 %fusion.2 = f32[96,2048]{1,0:T(8,128)} fusion(bf16[96,2048]{1,0:T(8,128)(2,1)S(1)} %bitcast.9, bf16[2048,2048]{1,0:T(8,128)(2,1)} %param.4), kind=kOutput, calls=%fused_computation.11 | convolution fusion | flops 805306368 | bytes 9568256 | tf_op jit(solution)/shard_map/dot_general | solution.py:25
  13.9 0.0 reduce-scatter.6.cloned.1.call-update
  13.9 0.0 copy-done.2
  14.0 28.9 %reduce-scatter.6.cloned.1.call-done = f32[24,2048]{1,0:T(8,128)} async-done(((f32[96,2048]{1,0:T(8,128)}), f32[24,2048]{1,0:T(8,128)}) %reduce-scatter.6.cloned.1.call-update) | async-done | bytes 196624
  42.9 1.1 reduce_max.9
  44.0 16.3 %pmax.7 = f32[24]{0:T(128)S(1)} all-reduce(f32[24]{0:T(128)S(1)} %reduce_max.9), channel_id=1, replica_groups=mesh['pair'=2,'dp'=2,'vocab'=8] {'vocab'}, use_global_device_ids=true, to_apply=%region_2.0 | all-reduce | flops 24 | bytes 192 | tf_op jit(solution)/shard_map/pmax | solution.py:31
  60.3 1.1 exponential_reduce_fusion
  61.4 13.6 %psum.14 = f32[24]{0:T(128)S(1)} all-reduce(f32[24]{0:T(128)S(1)} %exponential_reduce_fusion), channel_id=1, replica_groups=mesh['pair'=2,'dp'=2,'vocab'=8] {'vocab'}, use_global_device_ids=true, to_apply=%region_4.0 | all-reduce | flops 24 | bytes 192 | tf_op jit(solution)/shard_map/psum | solution.py:32
  75.0 1.0 broadcast_subtract_fusion
  76.0 1.5 collective-permute-start
  77.5 0.1 dynamic_slice.6
  77.6 0.0 copy-done.1
  77.6 0.6 dynamic-slice.6
  78.9 3.9 %collective-permute-done = f32[24,2048]{1,0:T(8,128)S(1)} collective-permute-done((f32[24,2048]{1,0:T(8,128)S(1)}, f32[24,2048]{1,0:T(8,128)S(1)}, u32[]{:S(2)}, u32[]{:S(2)}) %collective-permute-start) | collective-permute-done | bytes 196640 | tf_op jit(solution)/shard_map/ppermute | solution.py:12
  82.8 1.2 multiply_reduce_fusion
  84.0 13.6 %psum.15 = f32[24]{0:T(128)S(1)} all-reduce(f32[24]{0:T(128)S(1)} %multiply_reduce_fusion), channel_id=1, replica_groups=mesh['pair'=2,'dp'=2,'vocab'=8] {'vocab'}, use_global_device_ids=true, to_apply=%region_6.7 | all-reduce | flops 24 | bytes 192 | tf_op jit(solution)/shard_map/psum | solution.py:38
  97.6 1.1 multiply_select_fusion
  98.7 11.2 %all_gather.3 = f32[96,2048]{1,0:T(8,128)S(1)} all-gather(f32[24,2048]{1,0:T(8,128)S(1)} %multiply_select_fusion), channel_id=1, replica_groups=mesh['pair'=2,'dp'=2,'vocab'=8] {'pair','dp'}, dimensions={0}, use_global_device_ids=true | all-gather | bytes 983040 | tf_op jit(solution)/shard_map/all_gather | solution.py:44
  109.8 10.1 %fusion.3 = f32[96,2048]{1,0:T(8,128)S(1)} fusion(f32[96,2048]{1,0:T(8,128)S(1)} %all_gather.3, bf16[2048,2048]{1,0:T(8,128)(2,1)} %param.4), kind=kOutput, calls=%fused_computation.12 | convolution fusion | flops 4831838208 | bytes 9961472 | tf_op jit(solution)/shard_map/dot_general | solution.py:43
  120.0 20.2 %fusion = f32[16,2048]{1,0:T(8,128)S(1)} fusion(f32[96,2048]{1,0:T(8,128)S(1)} %fusion.3), kind=kCustom, calls=%all-reduce-scatter | all-reduce-scatter fusion | flops 262145 | bytes 918016
  140.2 1.3 collective-permute-start.1
  141.5 1.3 collective-permute-start.2
  142.8 0.6 dynamic-slice_multiply_fusion
  143.4 1.9 %collective-permute-done.2 = f32[12,2048]{1,0:T(8,128)S(1)} collective-permute-done((f32[12,2048]{1,0:T(8,128)S(1)}, f32[12,2048]{1,0:T(8,128)S(1)}, u32[]{:S(2)}, u32[]{:S(2)}) %collective-permute-start.2) | collective-permute-done | bytes 98336
  145.3 0.0 collective-permute-done.1
  145.3 0.4 concatenate
  145.7 0.7 constant_dynamic-slice_fusion
  (4 shorter events, 0.0 us)
Async XLA Ops:
  7.2 1.0 copy-start
  7.2 35.7 %reduce-scatter.6.cloned.1.call-start = ((), (), s32[]{:S(2)}) async-start(), calls=%async_computation.1 | async-start | bytes 983040
  8.2 5.8 %copy-start.2 = (s32[48]{0:T(128)S(1)}, s32[48]{0:T(128)}, u32[]{:S(2)}) copy-start(s32[48]{0:T(128)} %param.5) | copy-start | bytes 580
  8.2 69.5 %copy-start.1 = (u32[32]{0:T(128)S(1)}, u32[32]{0:T(128)}, u32[]{:S(2)}) copy-start(u32[32]{0:T(128)} %constant.28) | copy-start | bytes 388
  76.0 6.8 %collective-permute-start = (f32[24,2048]{1,0:T(8,128)S(1)}, f32[24,2048]{1,0:T(8,128)S(1)}, u32[]{:S(2)}, u32[]{:S(2)}) collective-permute-start(f32[24,2048]{1,0:T(8,128)S(1)} %broadcast_subtract_fusion), channel_id=1, source_target_pairs={{0,16},{16,0},{1,17},{17,1},{2,18},{18,2},{3,19},{19,3},{4,20},{20... | collective-permute-start | bytes 589832 | tf_op jit(solution)/shard_map/ppermute | solution.py:12
  140.2 5.1 %collective-permute-start.1 = (f32[16,2048]{1,0:T(8,128)S(1)}, f32[16,2048]{1,0:T(8,128)S(1)}, u32[]{:S(2)}, u32[]{:S(2)}) collective-permute-start(f32[16,2048]{1,0:T(8,128)S(1)} %fusion), channel_id=1, source_target_pairs={{0,1},{1,2},{2,3},{3,4},{4,5},{5,6},{6,7},{8,9},{9,10},{10,11},{11... | collective-permute-start | bytes 393224
  141.5 3.8 %collective-permute-start.2 = (f32[12,2048]{1,0:T(8,128)S(1)}, f32[12,2048]{1,0:T(8,128)S(1)}, u32[]{:S(2)}, u32[]{:S(2)}) collective-permute-start(f32[12,2048]{1,0:T(8,128)S(1)} %slice), channel_id=1, source_target_pairs={{0,2},{1,3},{2,4},{3,5},{4,6},{5,7},{8,10},{9,11},{10,12},{11,13},... | collective-permute-start | bytes 294920
Sparse Core Ops, SparseCore 0:
  14.1 28.7 reduce-scatter.5
where the time goes:
time: 154 us; the launch traced here: 153 us
  blocking collectives  74.8 us (49%)
  waiting for transfers between devices  34.8 us (23%)
  matrix products  15.9 us (10%)
  between operations  14.8 us (10%)
  other arithmetic  6.07 us (4%)
  starting transfers between devices  4.13 us (3%)
  local copies, waits for them, and re-layouts  2.67 us (2%)
    unnamed x4, waiting for transfers between devices  30.9 us
    unnamed x1, blocking collectives  20.2 us
    pmax x1, blocking collectives, per_device(): row_top = lax.pmax(jnp.max(own_logits, axis=1), 'vocab')  16.3 us
    psum x1, blocking collectives, per_device(): lax.psum(jnp.sum(jnp.exp(own_logits - row_top[:, None]), axis=1), 'vocab')  13.6 us
    psum x1, blocking collectives, per_device(): lax.psum(jnp.sum(clean_prob * (clean_logp - adv_logp), axis=1), 'vocab')  13.6 us
    all_gather x1, blocking collectives, per_device(): lax.all_gather(logit_grad, ('pair', 'dp'), axis=0, tiled=True)  11.2 us
    dot_general x1, matrix products, per_device(): lax.dot_general(lax.all_gather(logit_grad, ('pair', 'dp'), axis=0, tiled=...  10.1 us
    dot_general x1, matrix products, per_device(): jnp.dot(flat, head_weight, preferred_element_type=jnp.float32)  5.74 us
  transfers between devices with their start and end apart: 4, of which 3 were waited for; matrix products, arithmetic and copies ran while one was open for 1% of the time, Pallas kernels for 0%

commit v1 on v0

v1 whole, which is shorter than its diff:
```python
import functools

import jax
import jax.numpy as jnp
from jax import lax
from jax.experimental import pallas as pl
from jax.experimental.pallas import tpu as pltpu
from jax.sharding import PartitionSpec as P

trades_scale = 6.0
MESH = pl.DeviceIdType.MESH
F32 = jnp.float32
BF16 = jnp.bfloat16


def merge(parts):
    top_c = functools.reduce(jnp.maximum, [p[0] for p in parts])
    top_a = functools.reduce(jnp.maximum, [p[3] for p in parts])
    total_c = total_a = cross = 0.0
    for m_c, s_c, t, m_a, s_a in parts:
        down_c, down_a = m_c - top_c, m_a - top_a
        e_c = jnp.exp(down_c)
        total_c += e_c * s_c
        total_a += jnp.exp(down_a) * s_a
        cross += e_c * (t + s_c * (down_c - down_a))
    return top_c, total_c, cross, top_a, total_a


def pack(stats):
    rows = stats[0].shape[0]
    lane = lax.broadcasted_iota(jnp.int32, (rows, 128), 1)
    out = jnp.zeros((rows, 128), F32)
    for j, s in enumerate(stats):
        out = jnp.where(lane == j, s, out)
    return out


def unpack(value):
    return tuple(value[:, j : j + 1] for j in range(5))


def kernel(
    n_pair, n_dp, n_v,
    h_ref, w_ref, mask_ref,
    grad_ref, kl_ref,
    wbuf, part, rs_in, gath, gbuf, st_a, st_b, acc, core_in, z_in, z_own, c2_in,
    w_sem, rs_s, rs_r, ag_s, ag_r, sa_s, sa_r, sb_s, sb_r, c1_s, c1_r, z_s, z_r, c2_s, c2_r,
):
    n_xy = n_pair * n_dp
    n_hi = n_v // 2
    rows, depth = h_ref.shape
    tokens = rows // 2
    cols = wbuf.shape[2]
    half = depth // 2
    block = rows // n_hi
    px, py, v = lax.axis_index("pair"), lax.axis_index("dp"), lax.axis_index("vocab")
    hi, lo = v // 2, v % 2

    shifts = [(i // n_dp, i % n_dp) for i in range(n_xy)]
    peers = [
        (lax.rem(px + sx, n_pair), lax.rem(py + sy, n_dp)) for sx, sy in shifts
    ]
    minus = [((-sx) % n_pair) * n_dp + (-sy) % n_dp for sx, sy in shifts]
    order = sorted(range(1, n_xy), key=lambda i: -(shifts[i][0] + shifts[i][1]))

    def xy_id(i):
        return (peers[i][0], peers[i][1], v)

    def v_id(j):
        return (px, py, lax.rem(v + j, n_v))

    partner = (px, py, hi * 2 + (1 - lo))

    def hi_id(j):
        return (px, py, lax.rem(hi + j, n_hi) * 2 + lo)

    loads = {}
    for i in order + [0]:
        q = peers[i][0] * n_dp + peers[i][1]
        loads[i] = pltpu.make_async_copy(
            w_ref.at[:, pl.ds(pl.multiple_of(q * cols, 128), cols)], wbuf.at[i], w_sem.at[i]
        )
        loads[i].start()

    barrier = pltpu.get_barrier_semaphore()
    for i in range(1, n_xy):
        pl.semaphore_signal(barrier, inc=1, device_id=xy_id(i), device_id_type=MESH)
    for j in range(1, n_v):
        pl.semaphore_signal(barrier, inc=1, device_id=v_id(j), device_id_type=MESH)

    def remote(src, dst, send, recv, to):
        return pltpu.make_async_remote_copy(
            src_ref=src, dst_ref=dst, send_sem=send, recv_sem=recv, device_id=to, device_id_type=MESH
        )

    rs = {}
    for n, i in enumerate(order + [0]):
        loads[i].wait()
        part[i] = jnp.dot(h_ref[...], wbuf[i], preferred_element_type=F32)
        if n == 0:
            pl.semaphore_wait(barrier, n_xy - 1 + n_v - 1)
        if i:
            rs[i] = remote(part.at[i], rs_in.at[i], rs_s.at[i], rs_r.at[i], xy_id(i))
            rs[i].start()
    own = part[0]
    for i in order[::-1]:
        rs[i].wait_recv()
        own = own + rs_in[i]
    gath[0] = own
    ag = {}
    for i in order:
        ag[i] = remote(gath.at[0], gath.at[i], ag_s.at[i], ag_r.at[i], xy_id(i))
        ag[i].start()

    l_c, l_a = own[:tokens], own[tokens:]
    m_c = jnp.max(l_c, axis=1, keepdims=True)
    m_a = jnp.max(l_a, axis=1, keepdims=True)
    l_c, l_a = l_c - m_c, l_a - m_a
    e_c = jnp.exp(l_c)
    st_a[0] = pack((
        m_c,
        jnp.sum(e_c, axis=1, keepdims=True),
        jnp.sum(e_c * (l_c - l_a), axis=1, keepdims=True),
        m_a,
        jnp.sum(jnp.exp(l_a), axis=1, keepdims=True),
    ))
    sa = {}
    for j in range(1, n_v):
        sa[j] = remote(st_a.at[0], st_a.at[j], sa_s.at[j], sa_r.at[j], v_id(j))
        sa[j].start()
    for j in range(1, n_v):
        sa[j].wait_recv()
    st_b[0] = pack(merge([unpack(st_a[j]) for j in range(n_v)]))
    sb = {}
    for i in order:
        sb[i] = remote(st_b.at[0], st_b.at[i], sb_s.at[i], sb_r.at[i], xy_id(i))
        sb[i].start()

    row_iota = lax.broadcasted_iota(jnp.int32, (tokens, tokens), 0)
    col_iota = lax.broadcasted_iota(jnp.int32, (tokens, tokens), 1)
    mask = jnp.sum(
        jnp.where(row_iota == col_iota, mask_ref[...].astype(F32), 0.0), axis=1, keepdims=True
    )
    weight = trades_scale * mask

    for i in order:
        sb[i].wait_recv()
    top_c, total_c, cross, top_a, total_a = merge([unpack(st_b[i]) for i in range(n_xy)])
    log_c, log_a = jnp.log(total_c), jnp.log(total_a)
    kl = cross / total_c - log_c + log_a
    group = kl_ref.shape[1]
    token = lax.broadcasted_iota(jnp.int32, (tokens, group), 0)
    place = lax.broadcasted_iota(jnp.int32, (tokens, group), 1) + py * group
    kl_ref[...] = jnp.sum(jnp.where(token == place, mask * kl, 0.0), axis=0, keepdims=True)

    step = min(512, half)
    near = pl.multiple_of(lo * half, 128)
    far = pl.multiple_of((1 - lo) * half, 128)
    for n, i in enumerate([0] + order[::-1]):
        if i:
            ag[i].wait_recv()
        x_c = (gath[i, :tokens] - top_c) - log_c
        x_a = (gath[i, tokens:] - top_a) - log_a
        p_c = jnp.exp(x_c)
        g_c = weight * p_c * (x_c - x_a - kl)
        g_a = weight * (jnp.exp(x_a) - p_c)
        for k, g in enumerate((g_c, g_a)):
            high = g.astype(BF16)
            gbuf[pl.ds(k * tokens, tokens), :] = high
            gbuf[pl.ds(rows + k * tokens, tokens), :] = (g - high.astype(F32)).astype(BF16)
        for side, start in ((1, far), (0, near)):
            for d in range(0, half, step):
                both = lax.dot_general(
                    gbuf[...],
                    wbuf[minus[i], pl.ds(pl.multiple_of(start + d, 128), step), :],
                    (((1,), (1,)), ((), ())),
                    preferred_element_type=F32,
                )
                both = both[:rows] + both[rows:]
                if n == 0:
                    acc[side, :, d : d + step] = both
                else:
                    acc[side, :, d : d + step] += both
            if side and n == n_xy - 1:
                c1 = remote(acc.at[1], core_in, c1_s, c1_r, partner)
                c1.start()

    c1.wait_recv()
    acc[0] += core_in[...]
    zs = {}
    for j in range(n_hi - 1, 0, -1):
        to = lax.rem(hi + j, n_hi)
        zs[j] = remote(
            acc.at[0, pl.ds(pl.multiple_of(to * block, 8), block)],
            z_in.at[j], z_s.at[j], z_r.at[j], hi_id(j),
        )
        zs[j].start()
    total = acc[0, pl.ds(pl.multiple_of(hi * block, 8), block), :]
    for j in range(1, n_hi):
        zs[j].wait_recv()
        total = total + z_in[j]
    z_own[...] = total
    c2 = remote(z_own, c2_in, c2_s, c2_r, partner)
    c2.start()
    c2.wait_recv()
    out = block // 2
    first = lo == 0
    mine = jnp.where(first, z_own[:out], z_own[out:])
    theirs = jnp.where(first, c2_in[:out], c2_in[out:])
    grad_ref[:, :half] = jnp.where(first, mine, theirs)
    grad_ref[:, half:] = jnp.where(first, theirs, mine)

    for i in order:
        rs[i].wait_send()
        ag[i].wait_send()
        sb[i].wait_send()
    for j in range(1, n_v):
        sa[j].wait_send()
    for j in range(1, n_hi):
        zs[j].wait_send()
    c1.wait_send()
    c2.wait_send()


def solution(mesh):
    n_pair, n_dp, n_v = (mesh.shape[a] for a in ("pair", "dp", "vocab"))
    n_xy, n_hi = n_pair * n_dp, n_v // 2

    def per_device(hidden, head_weight, answer_mask):
        tokens = hidden.shape[1]
        rows = 2 * tokens
        depth, slab = head_weight.shape
        cols = slab // n_xy
        half = depth // 2
        block = rows // n_hi
        dma = pltpu.SemaphoreType.DMA
        vmem = pl.BlockSpec(memory_space=pltpu.VMEM)
        grad, kl = pl.pallas_call(
            functools.partial(kernel, n_pair, n_dp, n_v),
            out_shape=(
                jax.ShapeDtypeStruct((rows // n_v, depth), F32),
                jax.ShapeDtypeStruct((1, tokens // n_dp), F32),
            ),
            in_specs=[vmem, pl.BlockSpec(memory_space=pl.ANY), vmem],
            out_specs=(vmem, vmem),
            scratch_shapes=[
                pltpu.VMEM((n_xy, depth, cols), BF16),
                pltpu.VMEM((n_xy, rows, cols), F32),
                pltpu.VMEM((n_xy, rows, cols), F32),
                pltpu.VMEM((n_xy, rows, cols), F32),
                pltpu.VMEM((2 * rows, cols), BF16),
                pltpu.VMEM((n_v, tokens, 128), F32),
                pltpu.VMEM((n_xy, tokens, 128), F32),
                pltpu.VMEM((2, rows, half), F32),
                pltpu.VMEM((rows, half), F32),
                pltpu.VMEM((n_hi, block, half), F32),
                pltpu.VMEM((block, half), F32),
                pltpu.VMEM((block, half), F32),
                dma((n_xy,)),
                dma((n_xy,)), dma((n_xy,)),
                dma((n_xy,)), dma((n_xy,)),
                dma((n_v,)), dma((n_v,)),
                dma((n_xy,)), dma((n_xy,)),
                dma, dma,
                dma((n_hi,)), dma((n_hi,)),
                dma, dma,
            ],
            compiler_params=pltpu.CompilerParams(
                collective_id=0, has_side_effects=True, vmem_limit_bytes=48 * 2**20
            ),
        )(hidden.reshape(rows, depth), head_weight, answer_mask.reshape(1, tokens))
        return grad, kl.reshape(-1)

    return jax.shard_map(
        per_device,
        mesh=mesh,
        in_specs=(P(None, None, ("pair", "dp")), P(("pair", "dp"), "vocab"), P()),
        out_specs=(P("vocab", ("pair", "dp")), P("dp")),
        check_vma=False,
    )
```

time: 154 us -> 47.2 us (0.31)
  blocking collectives: 74.8 us -> 0 us
  Pallas kernels: 0 us -> 43.6 us
  waiting for transfers between devices: 34.8 us -> 0 us
  matrix products: 15.9 us -> 0 us
  between operations: 14.8 us -> 0.65 us
  other arithmetic: 6.07 us -> 0 us
  starting transfers between devices: 4.13 us -> 0 us
    pallas_call x0 -> x1, Pallas kernels: none -> 43.6 us  [per_device(): pl.pallas_call(functools.partial(kernel, n_pair, n_dp, n_v), out_shape=(j...]
    unnamed x4 -> x0, waiting for transfers between devices: 30.9 us -> none
    psum x2 -> x0, blocking collectives: 27.2 us -> none  [the longest x1 13.6 us: per_device(): lax.psum(jnp.sum(jnp.exp(own_logits - row_top[:, None]), axis=1), 'vocab')]
    unnamed x1 -> x0, blocking collectives: 20.2 us -> none
    pmax x1 -> x0, blocking collectives: 16.3 us -> none  [per_device(): row_top = lax.pmax(jnp.max(own_logits, axis=1), 'vocab')]
    dot_general x2 -> x0, matrix products: 15.9 us -> none  [the longest x1 10.1 us: per_device(): lax.dot_general(lax.all_gather(logit_grad, ('pair', 'dp'), axis=0, tiled=...]
    all_gather x1 -> x0, blocking collectives: 11.2 us -> none  [per_device(): lax.all_gather(logit_grad, ('pair', 'dp'), axis=0, tiled=True)]
    ppermute x1 -> x0, waiting for transfers between devices: 3.94 us -> none  [from_partner(): return lax.ppermute(value, axis, pairs)]
  transfers between devices with their start and end apart: 4 -> 0, of which waited for: 3 -> 0; matrix products, arithmetic and copies ran while one was open for 1% -> 0% of each run, Pallas kernels for 0% -> 0%
where the time goes in v1:
time: 47.2 us; the launch traced here: 47.1 us
  Pallas kernels  43.6 us (92%)
  local copies, waits for them, and re-layouts  2.81 us (6%)
  between operations  0.65 us (1%)
    pallas_call x1, Pallas kernels, per_device(): pl.pallas_call(functools.partial(kernel, n_pair, n_dp, n_v), out_shape=(j...  43.6 us
    unnamed x6, local copies, waits for them, and re-layouts  2.81 us

profile of v1, /device:TPU:0, one launch (start us, length us, event | category | flops | bytes accessed | tf_op | source)
XLA Modules:
  0.0 47.1 jit_solution(5710718874987104041)
XLA Ops:
  0.6 0.0 copy-start
  0.6 1.0 %copy-done = bf16[2,48,2048]{2,1,0:T(8,128)(2,1)S(1)} copy-done((bf16[2,48,2048]{2,1,0:T(8,128)(2,1)S(1)}, bf16[2,48,2048]{2,1,0:T(8,128)(2,1)}, u32[]{:S(2)}) %copy-start) | copy-done | bytes 393240
  1.6 0.0 copy-start.1
  1.6 0.7 %copy-done.1 = s32[48]{0:T(128)S(1)} copy-done((s32[48]{0:T(128)S(1)}, s32[48]{0:T(128)}, u32[]{:S(2)}) %copy-start.1) | copy-done | bytes 216
  2.3 43.6 %shard_map.50 = (f32[12,2048]{1,0:T(8,128)S(1)}, f32[1,24]{1,0:T(1,128)S(1)}) custom-call(bf16[96,2048]{1,0:T(8,128)(2,1)S(1)} %bitcast.3, bf16[2048,2048]{1,0:T(8,128)(2,1)} %w_ref.1, s32[1,48]{1,0:T(1,128)S(1)} %bitcast.4), custom_call_target="tpu_custom_call" | custom-call | tf_op jit(solution)/shard_map/pallas_call | solution.py:238
  45.9 0.7 %copy.7 = f32[12,2048]{1,0:T(8,128)} copy(f32[12,2048]{1,0:T(8,128)S(1)} %get-tuple-element.8) | data formatting | bytes 196608
  46.6 0.5 %copy.8 = f32[24]{0:T(128)} copy(f32[24]{0:T(128)S(1)} %bitcast.5) | data formatting | bytes 192
Async XLA Ops:
  0.6 1.0 %copy-start = (bf16[2,48,2048]{2,1,0:T(8,128)(2,1)S(1)}, bf16[2,48,2048]{2,1,0:T(8,128)(2,1)}, u32[]{:S(2)}) copy-start(bf16[2,48,2048]{2,1,0:T(8,128)(2,1)} %param.3) | copy-start | bytes 1179652
  1.6 0.7 %copy-start.1 = (s32[48]{0:T(128)S(1)}, s32[48]{0:T(128)}, u32[]{:S(2)}) copy-start(s32[48]{0:T(128)} %param.5) | copy-start | bytes 580

commit v2 on v1

v2 whole, which is shorter than its diff:
```python
import functools

import jax
import jax.numpy as jnp
from jax import lax
from jax.experimental import pallas as pl
from jax.experimental.pallas import tpu as pltpu
from jax.sharding import PartitionSpec as P

trades_scale = 6.0
MESH = pl.DeviceIdType.MESH
F32 = jnp.float32
BF16 = jnp.bfloat16


def merge(parts):
    top_c = functools.reduce(jnp.maximum, [p[0] for p in parts])
    top_a = functools.reduce(jnp.maximum, [p[3] for p in parts])
    total_c = total_a = cross = 0.0
    for m_c, s_c, t, m_a, s_a in parts:
        down_c, down_a = m_c - top_c, m_a - top_a
        e_c = jnp.exp(down_c)
        total_c += e_c * s_c
        total_a += jnp.exp(down_a) * s_a
        cross += e_c * (t + s_c * (down_c - down_a))
    return top_c, total_c, cross, top_a, total_a


def pack(stats):
    place = lax.broadcasted_iota(jnp.int32, (8, stats[0].shape[1]), 0)
    out = jnp.zeros(place.shape, F32)
    for j, s in enumerate(stats):
        out = jnp.where(place == j, s, out)
    return out


def unpack(value):
    return tuple(value[j : j + 1, :] for j in range(5))


def kernel(
    n_pair, n_dp, n_v,
    h_any, w_ref, mask_any,
    grad_ref, kl_ref,
    h_ref, mask_ref, wbuf, part, rs_in, gath, gbuf, st_a, st_b, acc, core_in, z_in, z_own, c2_in,
    w_sem, in_sem, rs_s, rs_r, ag_s, ag_r, sa_s, sa_r, sb_s, sb_r, c1_s, c1_r, z_s, z_r, c2_s, c2_r,
):
    n_xy = n_pair * n_dp
    n_hi = n_v // 2
    rows, depth = h_ref.shape
    tokens = rows // 2
    few = tokens // 2
    wide = st_a.shape[2]
    cols = wbuf.shape[2]
    half = depth // 2
    block = rows // n_hi
    px, py, v = lax.axis_index("pair"), lax.axis_index("dp"), lax.axis_index("vocab")
    hi, lo = v // 2, v % 2

    shifts = [(i // n_dp, i % n_dp) for i in range(n_xy)]
    peers = [
        (lax.rem(px + sx, n_pair), lax.rem(py + sy, n_dp)) for sx, sy in shifts
    ]
    minus = [((-sx) % n_pair) * n_dp + (-sy) % n_dp for sx, sy in shifts]
    along_x = [sx * n_dp for sx in range(1, n_pair)]
    along_y = list(range(1, n_dp))
    across = [i for i in range(n_xy) if shifts[i][0] and shifts[i][1]]
    order = across + along_x + along_y + [0]

    def xy_id(i):
        return (peers[i][0], peers[i][1], v)

    def v_id(j):
        return (px, py, lax.rem(v + j, n_v))

    partner = (px, py, hi * 2 + (1 - lo))

    h_load = pltpu.make_async_copy(h_any, h_ref, in_sem.at[0])
    h_load.start()
    loads = {}
    for i in order:
        q = peers[i][0] * n_dp + peers[i][1]
        loads[i] = pltpu.make_async_copy(
            w_ref.at[:, pl.ds(pl.multiple_of(q * cols, 128), cols)], wbuf.at[i], w_sem.at[i]
        )
        loads[i].start()
    mask_load = pltpu.make_async_copy(mask_any, mask_ref, in_sem.at[1])
    mask_load.start()

    barrier = pltpu.get_barrier_semaphore()
    for i in range(1, n_xy):
        pl.semaphore_signal(barrier, inc=1, device_id=xy_id(i), device_id_type=MESH)
    for j in range(1, n_v):
        pl.semaphore_signal(barrier, inc=1, device_id=v_id(j), device_id_type=MESH)

    def remote(src, dst, send, recv, to):
        copy = pltpu.make_async_remote_copy(
            src_ref=src, dst_ref=dst, send_sem=send, recv_sem=recv, device_id=to, device_id_type=MESH
        )
        copy.start()
        return copy

    rs = {}

    def reduce_send(g, i, to):
        rs[g, i] = remote(part.at[g, i], rs_in.at[g, i], rs_s.at[g, i], rs_r.at[g, i], xy_id(to))

    h_load.wait()
    for n, i in enumerate(order):
        sx, sy = shifts[i]
        loads[i].wait()
        value = jnp.dot(h_ref[...], wbuf[i], preferred_element_type=F32)
        for g in range(2):
            for k in range(2):
                part[g, i, k] = value[k * tokens + g * few : k * tokens + (g + 1) * few]
        if n == 0:
            pl.semaphore_wait(barrier, n_xy - 1 + n_v - 1)
        if sx:
            reduce_send(0, i, sx * n_dp)
        if sy:
            reduce_send(1, i, sy)

    def take(g, i, source):
        rs[g, source].wait_recv()
        part[g, i] += rs_in[g, source]

    for sy in along_y:
        for sx in range(1, n_pair):
            take(0, sy, sx * n_dp + sy)
        reduce_send(0, sy, sy)
    for i in along_x:
        for sy in along_y:
            take(1, i, i + sy)
        reduce_send(1, i, i)

    ag = {}

    def gather_send(g):
        for i in along_x + along_y:
            ag[g, i, 0] = remote(
                gath.at[g, 0], gath.at[g, i], ag_s.at[g, i, 0], ag_r.at[g, i, 0], xy_id(i)
            )

    def gather_forward(g):
        for sy in along_y:
            ag[g, sy, 0].wait_recv()
            for i in along_x:
                ag[g, i + sy, 0] = remote(
                    gath.at[g, sy, 0], gath.at[g, i + sy, 0],
                    ag_s.at[g, i + sy, 0], ag_r.at[g, i + sy, 0], xy_id(i),
                )
        for i in along_x:
            ag[g, i, 0].wait_recv()
            for sy in along_y:
                ag[g, i + sy, 1] = remote(
                    gath.at[g, i, 1], gath.at[g, i + sy, 1],
                    ag_s.at[g, i + sy, 1], ag_r.at[g, i + sy, 1], xy_id(sy),
                )

    for i in along_x:
        take(0, 0, i)
    for i in along_y:
        take(1, 0, i)
    for i in along_y:
        rs[0, i].wait_recv()
    gath[0, 0] = part[0, 0] + sum(rs_in[0, i] for i in along_y)
    gather_send(0)
    for i in along_x:
        rs[1, i].wait_recv()
    gath[1, 0] = part[1, 0] + sum(rs_in[1, i] for i in along_x)

    diagonal = lax.broadcasted_iota(jnp.int32, (tokens, wide), 0) == lax.broadcasted_iota(
        jnp.int32, (tokens, wide), 1
    )

    def to_row(column):
        return jnp.sum(jnp.where(diagonal, column, 0.0), axis=0, keepdims=True)

    def to_column(row):
        return jnp.sum(jnp.where(diagonal, row, 0.0), axis=1, keepdims=True)

    l_c = jnp.concatenate([gath[0, 0, 0], gath[1, 0, 0]], axis=0)
    l_a = jnp.concatenate([gath[0, 0, 1], gath[1, 0, 1]], axis=0)
    m_c = jnp.max(l_c, axis=1, keepdims=True)
    m_a = jnp.max(l_a, axis=1, keepdims=True)
    l_c, l_a = l_c - m_c, l_a - m_a
    e_c = jnp.exp(l_c)
    stats = (
        m_c,
        jnp.sum(e_c, axis=1, keepdims=True),
        jnp.sum(e_c * (l_c - l_a), axis=1, keepdims=True),
        m_a,
        jnp.sum(jnp.exp(l_a), axis=1, keepdims=True),
    )
    st_a[0] = pack([to_row(s) for s in stats])
    sa = {}
    for j in range(1, n_v):
        sa[j] = remote(st_a.at[0], st_a.at[j], sa_s.at[j], sa_r.at[j], v_id(j))
    for j in range(1, n_v):
        sa[j].wait_recv()
    st_b[0] = pack(merge([unpack(st_a[j]) for j in range(n_v)]))
    sb = {}
    for i in range(1, n_xy):
        sb[i] = remote(st_b.at[0], st_b.at[i], sb_s.at[i], sb_r.at[i], xy_id(i))
    gather_forward(0)
    gather_send(1)

    mask_load.wait()
    mask = jnp.sum(
        jnp.where(diagonal[:, :tokens], mask_ref[...].astype(F32), 0.0), axis=1, keepdims=True
    )
    weight = trades_scale * mask
    for i in range(1, n_xy):
        sb[i].wait_recv()
    joined = merge([unpack(st_b[i]) for i in range(n_xy)])
    top_c, total_c, cross, top_a, total_a = (to_column(s) for s in joined)
    log_c, log_a = jnp.log(total_c), jnp.log(total_a)
    kl = cross / total_c - log_c + log_a
    group = kl_ref.shape[1]
    token = lax.broadcasted_iota(jnp.int32, (tokens, group), 0)
    place = lax.broadcasted_iota(jnp.int32, (tokens, group), 1) + py * group
    kl_ref[...] = jnp.sum(jnp.where(token == place, mask * kl, 0.0), axis=0, keepdims=True)

    step = min(512, half)
    near = pl.multiple_of(lo * half, 128)
    far = pl.multiple_of((1 - lo) * half, 128)

    def product(g):
        mine = slice(g * few, (g + 1) * few)
        for n, i in enumerate([0] + along_y + along_x + across):
            if i in across:
                ag[g, i, 0].wait_recv()
                ag[g, i, 1].wait_recv()
            x_c = (gath[g, i, 0] - top_c[mine]) - log_c[mine]
            x_a = (gath[g, i, 1] - top_a[mine]) - log_a[mine]
            p_c = jnp.exp(x_c)
            g_c = weight[mine] * p_c * (x_c - x_a - kl[mine])
            g_a = weight[mine] * (jnp.exp(x_a) - p_c)
            both = jnp.concatenate([g_c, g_a], axis=0)
            high = both.astype(BF16)
            slot = n % 2
            gbuf[slot, :tokens] = high
            gbuf[slot, tokens:] = (both - high.astype(F32)).astype(BF16)
            for side, start in ((1, far), (0, near)):
                for d in range(0, half, step):
                    out = lax.dot_general(
                        gbuf[slot],
                        wbuf[minus[i], pl.ds(pl.multiple_of(start + d, 128), step), :],
                        (((1,), (1,)), ((), ())),
                        preferred_element_type=F32,
                    )
                    out = out[:tokens] + out[tokens:]
                    if n == 0:
                        acc[g, side, :, d : d + step] = out
                    else:
                        acc[g, side, :, d : d + step] += out
                if side and n == n_xy - 1:
                    c1[g] = remote(acc.at[g, 1], core_in.at[g], c1_s.at[g], c1_r.at[g], partner)

    places = [
        (k * (n_hi // 2) + g * (n_hi // 4) + b, g, k * few + b * block)
        for g in range(2) for k in range(2) for b in range(n_hi // 4)
    ]

    def z_copy(to, g, row):
        return pltpu.make_async_remote_copy(
            src_ref=acc.at[g, 0, pl.ds(row, block)],
            dst_ref=z_in.at[hi],
            send_sem=z_s.at[to],
            recv_sem=z_r.at[hi],
            device_id=(px, py, to * 2 + lo),
            device_id_type=MESH,
        )

    def z_send(g):
        c1[g].wait_recv()
        acc[g, 0] += core_in[g]
        for to, which, row in places:
            if which == g:
                @pl.when(hi != to)
                def _():
                    z_copy(to, g, row).start()

                @pl.when(hi == to)
                def _():
                    z_in[to] = acc[g, 0, pl.ds(row, block), :]

    c1 = {}
    product(0)
    gather_forward(1)
    z_send(0)
    product(1)
    z_send(1)
    for source in range(n_hi):
        @pl.when(hi != source)
        def _():
            pltpu.make_async_remote_copy(
                src_ref=z_in.at[source], dst_ref=z_in.at[source],
                send_sem=z_s.at[source], recv_sem=z_r.at[source],
                device_id=(px, py, source * 2 + lo), device_id_type=MESH,
            ).wait_recv()
    z_own[...] = sum(z_in[j] for j in range(n_hi))
    c2 = remote(z_own, c2_in, c2_s, c2_r, partner)
    c2.wait_recv()
    out = block // 2
    first = lo == 0
    mine = jnp.where(first, z_own[:out], z_own[out:])
    theirs = jnp.where(first, c2_in[:out], c2_in[out:])
    grad_ref[:, :half] = jnp.where(first, mine, theirs)
    grad_ref[:, half:] = jnp.where(first, theirs, mine)

    for copy in [*rs.values(), *ag.values(), *sa.values(), *sb.values(), *c1.values(), c2]:
        copy.wait_send()
    for to, g, row in places:
        @pl.when(hi != to)
        def _():
            z_copy(to, g, row).wait_send()


def solution(mesh):
    n_pair, n_dp, n_v = (mesh.shape[a] for a in ("pair", "dp", "vocab"))
    n_xy, n_hi = n_pair * n_dp, n_v // 2

    def per_device(hidden, head_weight, answer_mask):
        tokens = hidden.shape[1]
        rows, few = 2 * tokens, tokens // 2
        depth, slab = head_weight.shape
        cols = slab // n_xy
        half = depth // 2
        block = rows // n_hi
        wide = -(-tokens // 128) * 128
        dma = pltpu.SemaphoreType.DMA
        vmem = pl.BlockSpec(memory_space=pltpu.VMEM)
        anywhere = pl.BlockSpec(memory_space=pl.ANY)
        grad, kl = pl.pallas_call(
            functools.partial(kernel, n_pair, n_dp, n_v),
            out_shape=(
                jax.ShapeDtypeStruct((rows // n_v, depth), F32),
                jax.ShapeDtypeStruct((1, tokens // n_dp), F32),
            ),
            in_specs=[anywhere] * 3,
            out_specs=(vmem, vmem),
            scratch_shapes=[
                pltpu.VMEM((rows, depth), BF16),
                pltpu.VMEM((1, tokens), jnp.int32),
                pltpu.VMEM((n_xy, depth, cols), BF16),
                pltpu.VMEM((2, n_xy, 2, few, cols), F32),
                pltpu.VMEM((2, n_xy, 2, few, cols), F32),
                pltpu.VMEM((2, n_xy, 2, few, cols), F32),
                pltpu.VMEM((2, rows, cols), BF16),
                pltpu.VMEM((n_v, 8, wide), F32),
                pltpu.VMEM((n_xy, 8, wide), F32),
                pltpu.VMEM((2, 2, tokens, half), F32),
                pltpu.VMEM((2, tokens, half), F32),
                pltpu.VMEM((n_hi, block, half), F32),
                pltpu.VMEM((block, half), F32),
                pltpu.VMEM((block, half), F32),
                dma((n_xy,)), dma((2,)),
                dma((2, n_xy)), dma((2, n_xy)),
                dma((2, n_xy, 2)), dma((2, n_xy, 2)),
                dma((n_v,)), dma((n_v,)),
                dma((n_xy,)), dma((n_xy,)),
                dma((2,)), dma((2,)),
                dma((n_hi,)), dma((n_hi,)),
                dma, dma,
            ],
            compiler_params=pltpu.CompilerParams(
                collective_id=0, has_side_effects=True, vmem_limit_bytes=48 * 2**20
            ),
        )(hidden.reshape(rows, depth), head_weight, answer_mask.reshape(1, tokens))
        return grad, kl.reshape(-1)

    return jax.shard_map(
        per_device,
        mesh=mesh,
        in_specs=(P(None, None, ("pair", "dp")), P(("pair", "dp"), "vocab"), P()),
        out_specs=(P("vocab", ("pair", "dp")), P("dp")),
        check_vma=False,
    )
```

time: 47.2 us -> 40.2 us (0.85)
  the two profiles are of different devices: /device:TPU:0 before, /device:TPU:25 now
where the time goes in v2:
time: 40.2 us; the launch traced here: 40 us
  Pallas kernels  36.5 us (91%)
  local copies, waits for them, and re-layouts  2.81 us (7%)
  between operations  0.65 us (2%)
    pallas_call x1, Pallas kernels, per_device(): pl.pallas_call(functools.partial(kernel, n_pair, n_dp, n_v), out_shape=(j...  36.5 us
    unnamed x6, local copies, waits for them, and re-layouts  2.81 us

profile of v2, /device:TPU:25, one launch (start us, length us, event | category | flops | bytes accessed | tf_op | source)
XLA Modules:
  0.0 40.0 jit_solution(16251051332666396863)
XLA Ops:
  0.6 0.0 copy-start
  0.6 1.0 %copy-done = bf16[2,48,2048]{2,1,0:T(8,128)(2,1)S(1)} copy-done((bf16[2,48,2048]{2,1,0:T(8,128)(2,1)S(1)}, bf16[2,48,2048]{2,1,0:T(8,128)(2,1)}, u32[]{:S(2)}) %copy-start) | copy-done | bytes 393240
  1.6 0.0 copy-start.1
  1.6 0.7 %copy-done.1 = s32[48]{0:T(128)S(1)} copy-done((s32[48]{0:T(128)S(1)}, s32[48]{0:T(128)}, u32[]{:S(2)}) %copy-start.1) | copy-done | bytes 216
  2.3 36.5 %shard_map.50 = (f32[12,2048]{1,0:T(8,128)S(1)}, f32[1,24]{1,0:T(1,128)S(1)}) custom-call(bf16[96,2048]{1,0:T(8,128)(2,1)S(1)} %bitcast.3, bf16[2048,2048]{1,0:T(8,128)(2,1)} %w_ref.1, s32[1,48]{1,0:T(1,128)S(1)} %bitcast.4), custom_call_target="tpu_custom_call" | custom-call | tf_op jit(solution)/shard_map/pallas_call | solution.py:335
  38.8 0.7 %copy.7 = f32[12,2048]{1,0:T(8,128)} copy(f32[12,2048]{1,0:T(8,128)S(1)} %get-tuple-element.8) | data formatting | bytes 196608
  39.5 0.5 %copy.8 = f32[24]{0:T(128)} copy(f32[24]{0:T(128)S(1)} %bitcast.5) | data formatting | bytes 192
Async XLA Ops:
  0.6 1.0 %copy-start = (bf16[2,48,2048]{2,1,0:T(8,128)(2,1)S(1)}, bf16[2,48,2048]{2,1,0:T(8,128)(2,1)}, u32[]{:S(2)}) copy-start(bf16[2,48,2048]{2,1,0:T(8,128)(2,1)} %param.3) | copy-start | bytes 1179652
  1.6 0.7 %copy-start.1 = (s32[48]{0:T(128)S(1)}, s32[48]{0:T(128)}, u32[]{:S(2)}) copy-start(s32[48]{0:T(128)} %param.5) | copy-start | bytes 580

commit v3 on v2

--- a/solution.py
+++ b/solution.py
@@ -254,36 +254,41 @@
                         acc[g, side, :, d : d + step] = out
                     else:
                         acc[g, side, :, d : d + step] += out
-                if side and n == n_xy - 1:
-                    c1[g] = remote(acc.at[g, 1], core_in.at[g], c1_s.at[g], c1_r.at[g], partner)
+                    if side and n == n_xy - 1:
+                        c1[g, d] = remote(
+                            acc.at[g, 1, :, pl.ds(d, step)], core_in.at[g, :, pl.ds(d, step)],
+                            c1_s.at[g, d // step], c1_r.at[g, d // step], partner,
+                        )
 
     places = [
         (k * (n_hi // 2) + g * (n_hi // 4) + b, g, k * few + b * block)
         for g in range(2) for k in range(2) for b in range(n_hi // 4)
     ]
-
-    def z_copy(to, g, row):
+    places.sort(key=lambda place: min(place[0], n_hi - 1 - place[0]))
+
+    def z_copy(to, g, row, d):
         return pltpu.make_async_remote_copy(
-            src_ref=acc.at[g, 0, pl.ds(row, block)],
-            dst_ref=z_in.at[hi],
-            send_sem=z_s.at[to],
-            recv_sem=z_r.at[hi],
+            src_ref=acc.at[g, 0, pl.ds(row, block), pl.ds(d, step)],
+            dst_ref=z_in.at[hi, :, pl.ds(d, step)],
+            send_sem=z_s.at[to, d // step],
+            recv_sem=z_r.at[hi, d // step],
             device_id=(px, py, to * 2 + lo),
             device_id_type=MESH,
         )
 
     def z_send(g):
-        c1[g].wait_recv()
-        acc[g, 0] += core_in[g]
-        for to, which, row in places:
-            if which == g:
-                @pl.when(hi != to)
-                def _():
-                    z_copy(to, g, row).start()
-
-                @pl.when(hi == to)
-                def _():
-                    z_in[to] = acc[g, 0, pl.ds(row, block), :]
+        for d in range(0, half, step):
+            c1[g, d].wait_recv()
+            acc[g, 0, :, d : d + step] += core_in[g, :, d : d + step]
+            for to, which, row in places:
+                if which == g:
+                    @pl.when(hi != to)
+                    def _():
+                        z_copy(to, g, row, d).start()
+
+                    @pl.when(hi == to)
+                    def _():
+                        z_in[to, :, d : d + step] = acc[g, 0, pl.ds(row, block), d : d + step]
 
     c1 = {}
     product(0)
@@ -291,12 +296,12 @@
     z_send(0)
     product(1)
     z_send(1)
-    for source in range(n_hi):
+    for source, d in [(j, d) for j in range(n_hi) for d in range(0, half, step)]:
         @pl.when(hi != source)
         def _():
             pltpu.make_async_remote_copy(
-                src_ref=z_in.at[source], dst_ref=z_in.at[source],
-                send_sem=z_s.at[source], recv_sem=z_r.at[source],
+                src_ref=z_in.at[source, :, pl.ds(d, step)], dst_ref=z_in.at[source, :, pl.ds(d, step)],
+                send_sem=z_s.at[source, d // step], recv_sem=z_r.at[source, d // step],
                 device_id=(px, py, source * 2 + lo), device_id_type=MESH,
             ).wait_recv()
     z_own[...] = sum(z_in[j] for j in range(n_hi))
@@ -314,7 +319,8 @@
     for to, g, row in places:
         @pl.when(hi != to)
         def _():
-            z_copy(to, g, row).wait_send()
+            for d in range(0, half, step):
+                z_copy(to, g, row, d).wait_send()
 
 
 def solution(mesh):
@@ -328,6 +334,7 @@
         cols = slab // n_xy
         half = depth // 2
         block = rows // n_hi
+        pieces = half // min(512, half)
         wide = -(-tokens // 128) * 128
         dma = pltpu.SemaphoreType.DMA
         vmem = pl.BlockSpec(memory_space=pltpu.VMEM)
@@ -360,8 +367,8 @@
                 dma((2, n_xy, 2)), dma((2, n_xy, 2)),
                 dma((n_v,)), dma((n_v,)),
                 dma((n_xy,)), dma((n_xy,)),
-                dma((2,)), dma((2,)),
-                dma((n_hi,)), dma((n_hi,)),
+                dma((2, pieces)), dma((2, pieces)),
+                dma((n_hi, pieces)), dma((n_hi, pieces)),
                 dma, dma,
             ],
             compiler_params=pltpu.CompilerParams(

time: 40.2 us -> 40.1 us (level)
  no operation moved by 1% of the time
where the time goes in v3:
time: 40.1 us; the launch traced here: 40 us
  Pallas kernels  36.5 us (91%)
  local copies, waits for them, and re-layouts  2.81 us (7%)
  between operations  0.65 us (2%)
    pallas_call x1, Pallas kernels, per_device(): pl.pallas_call(functools.partial(kernel, n_pair, n_dp, n_v), out_shape=(j...  36.5 us
    unnamed x6, local copies, waits for them, and re-layouts  2.81 us

profile of v3, /device:TPU:25, one launch (start us, length us, event | category | flops | bytes accessed | tf_op | source)
XLA Modules:
  0.0 40.0 jit_solution(11041907569107862407)
XLA Ops:
  0.6 0.0 copy-start
  0.6 1.0 %copy-done = bf16[2,48,2048]{2,1,0:T(8,128)(2,1)S(1)} copy-done((bf16[2,48,2048]{2,1,0:T(8,128)(2,1)S(1)}, bf16[2,48,2048]{2,1,0:T(8,128)(2,1)}, u32[]{:S(2)}) %copy-start) | copy-done | bytes 393240
  1.6 0.0 copy-start.1
  1.6 0.7 %copy-done.1 = s32[48]{0:T(128)S(1)} copy-done((s32[48]{0:T(128)S(1)}, s32[48]{0:T(128)}, u32[]{:S(2)}) %copy-start.1) | copy-done | bytes 216
  2.3 36.5 %shard_map.50 = (f32[12,2048]{1,0:T(8,128)S(1)}, f32[1,24]{1,0:T(1,128)S(1)}) custom-call(bf16[96,2048]{1,0:T(8,128)(2,1)S(1)} %bitcast.3, bf16[2048,2048]{1,0:T(8,128)(2,1)} %w_ref.1, s32[1,48]{1,0:T(1,128)S(1)} %bitcast.4), custom_call_target="tpu_custom_call" | custom-call | tf_op jit(solution)/shard_map/pallas_call | solution.py:342
  38.8 0.7 %copy.7 = f32[12,2048]{1,0:T(8,128)} copy(f32[12,2048]{1,0:T(8,128)S(1)} %get-tuple-element.8) | data formatting | bytes 196608
  39.4 0.5 %copy.8 = f32[24]{0:T(128)} copy(f32[24]{0:T(128)S(1)} %bitcast.5) | data formatting | bytes 192
Async XLA Ops:
  0.6 1.0 %copy-start = (bf16[2,48,2048]{2,1,0:T(8,128)(2,1)S(1)}, bf16[2,48,2048]{2,1,0:T(8,128)(2,1)}, u32[]{:S(2)}) copy-start(bf16[2,48,2048]{2,1,0:T(8,128)(2,1)} %param.3) | copy-start | bytes 1179652
  1.6 0.7 %copy-start.1 = (s32[48]{0:T(128)S(1)}, s32[48]{0:T(128)}, u32[]{:S(2)}) copy-start(s32[48]{0:T(128)} %param.5) | copy-start | bytes 580
